TPU v7x, 32 devices: a whole 2x2x4 slice. The times are simulated.
32 devices in a mesh: dp: 4 (over y, x), tensor: 8 (over z, core).
Axes of the slice: x: 2, y: 2, z: 4, core: 2. Of those that a mesh axis runs over, the one named last changes fastest.
Arguments:
- hidden: bfloat16 [8192, 2048], P(('dp', 'tensor')), may hold values from -6 to 6
- norm_gain: float32 [2048], replicated, may hold values from 0.5 to 1.5
- head_weight: bfloat16 [2048, 102400], P('dp', 'tensor'), as said below
- token_ids: int32 [8192], P(('dp', 'tensor')), may hold values from 0 to 102399
- lengths: int32 [4, 4], P('dp'), may hold values from 1 to 512, 1024 in all within a row
Outputs:
- logprob: float32 [8192], P(('dp', 'tensor'))
- entropy: float32 [8192], P(('dp', 'tensor'))
Inputs may be any that keep to these rules, and one draw needn't show every extreme that they name: Each index of dp has 4 lengths that sum to exactly 1024, and one of them equals 512. `head_weight`: head weights.
All inputs are finite; a program needn't handle non-finite values.
Results may differ from a plain program's by a relative error of at most 0.0045.
Values may be sent and summed in bfloat16 or wider, within the bound.
A program may use at most 256 MiB of HBM per device.

v0:
```python
import jax
import jax.numpy as jnp
from jax import lax
from jax.sharding import PartitionSpec as P

SEQ_DP = 4
SLOT = 512


def per_device(hidden, norm_gain, head_weight, token_ids, lengths):
    row_dev = hidden.shape[0]
    tensor_idx = lax.axis_index("tensor")
    wide = hidden.astype(jnp.float32)
    meansq = jnp.mean(wide * wide, axis=-1, keepdims=True)
    normed = (wide * lax.rsqrt(meansq + 1e-06) * norm_gain).astype(jnp.bfloat16)
    weight = lax.all_gather(head_weight, "dp", axis=0, tiled=True)
    vocab_dev = weight.shape[1]
    vstart = tensor_idx * vocab_dev
    seq_len = lengths[0]
    seq_iota = jnp.arange(SEQ_DP, dtype=jnp.int32)
    vocab_iota = jnp.arange(vocab_dev, dtype=jnp.int32)
    own_rows = tensor_idx * row_dev + jnp.arange(row_dev, dtype=jnp.int32)
    logits = jnp.dot(
        lax.all_gather(normed, "tensor", axis=0, tiled=True),
        weight,
        preferred_element_type=jnp.float32,
    )
    top = jnp.max(logits, axis=1)
    expo = jnp.exp(logits - top[:, None])
    total = jnp.sum(expo, axis=1)
    moment = jnp.sum(expo * logits, axis=1)
    hit = (lax.all_gather(token_ids, "tensor", axis=0, tiled=True) - vstart)[:, None] == vocab_iota[
        None, :
    ]
    chosen = jnp.sum(jnp.where(hit, logits, 0.0), axis=1)
    fresh = (top, total, moment, chosen)
    top, total, moment, chosen = tuple((new for new in fresh))
    onehot = (own_rows // SLOT)[:, None] == seq_iota[None, :]
    length_of = jnp.sum(jnp.where(onehot, seq_len[None, :], 0), axis=1)
    within = own_rows % SLOT
    scored = within < length_of
    top_all = lax.pmax(top, "tensor")
    rescale = jnp.exp(top - top_all)
    top_own = top_all[own_rows]
    total_all, moment_all, chosen_all = lax.psum(
        (total * rescale, moment * rescale, chosen), "tensor"
    )
    total_own, moment_own, chosen_own = (
        total_all[own_rows],
        moment_all[own_rows],
        chosen_all[own_rows],
    )
    safe_total = jnp.where(scored, total_own, 1.0)
    lse = top_own + jnp.log(safe_total)
    logprob = jnp.where(scored, chosen_own - lse, 0.0)
    entropy = jnp.where(scored, lse - moment_own / safe_total, 0.0)
    return (logprob, entropy)


def solution(mesh):
    return jax.shard_map(
        per_device,
        mesh=mesh,
        in_specs=(
            P(("dp", "tensor"), None),
            P(),
            P("dp", "tensor"),
            P(("dp", "tensor")),
            P("dp", None),
        ),
        out_specs=(P(("dp", "tensor")), P(("dp", "tensor"))),
        check_vma=False,
    )
```

profile of v0, /device:TPU:0, one launch (start us, length us, event | category | flops | bytes accessed | tf_op | source)
XLA Modules:
  0.0 774.9 jit_solution(18076474057371873450)
XLA Ops:
  7.2 0.0 all-gather.4.cloned.1.call-start
  7.2 1.5 fusion.1
  8.7 2.5 fusion.3
  11.3 0.0 all-gather.4.cloned.1.call-update
  11.3 0.0 all-gather.6.cloned.1.call-start
  11.3 0.7 all-gather.6.cloned.1.call-update
  12.0 13.7 %all-gather = s32[8,1,256]{2,1,0:T(1,128)S(1)} all-gather(s32[1,1,256]{2,1,0:T(1,128)} %bitcast.10), channel_id=1, replica_groups=mesh['dp'=4,'tensor'=8] {'tensor'}, dimensions={0}, use_global_device_ids=true | all-gather | bytes 9216 | tf_op jit(solution)/shard_map/all_gather | solution.py:32
  25.7 0.6 pad_clamp_fusion
  26.3 1.3 select_reduce_fusion.1
  27.6 0.6 broadcast_subtract_fusion
  28.2 68.0 %all-gather.4.cloned.1.call-done = bf16[2048,2048]{1,0:T(8,128)(2,1)} async-done(((bf16[256,2048]{1,0:T(8,128)(2,1)}), bf16[2048,2048]{1,0:T(8,128)(2,1)}) %all-gather.4.cloned.1.call-update) | async-done | bytes 8388624 | tf_op jit(solution)/shard_map/all_gather | solution.py:24
  96.2 456.0 %all-gather.6.cloned.1.call-done = bf16[2048,12800]{1,0:T(8,128)(2,1)} async-done(((bf16[512,12800]{1,0:T(8,128)(2,1)}), bf16[2048,12800]{1,0:T(8,128)(2,1)}) %all-gather.6.cloned.1.call-update) | async-done | bytes 52428816 | tf_op jit(solution)/shard_map/all_gather | solution.py:16
  552.2 122.2 %fusion.8 = (f32[2048]{0:T(1024)S(1)}, f32[2048,12800]{1,0:T(8,128)}) fusion(bf16[2048,2048]{1,0:T(8,128)(2,1)} %all-gather.4.cloned.1.call-done, bf16[2048,12800]{1,0:T(8,128)(2,1)} %all-gather.6.cloned.1.call-done), kind=kOutput, calls=%fused_computation.35 | convolution fusion | flops 107400396800 | bytes 165683200 | tf_op jit(solution)/shard_map/dot_general | solution.py:23
  674.3 16.8 %pmax.7 = f32[2048]{0:T(1024)S(1)} all-reduce(f32[2048]{0:T(1024)S(1)} %get-tuple-element.12), channel_id=1, replica_groups=mesh['dp'=4,'tensor'=8] {'tensor'}, use_global_device_ids=true, to_apply=%region_5.6 | all-reduce | flops 2048 | bytes 16384 | tf_op jit(solution)/shard_map/pmax | solution.py:42
  691.1 0.0 copy-done
  691.1 0.0 copy-start.1
  691.1 0.0 copy-start.2
  691.1 43.4 %multiply_reduce_fusion = (f32[2048]{0:T(1024)S(1)}, f32[2048]{0:T(1024)S(1)}, f32[2048]{0:T(1024)S(1)}) fusion(f32[2048,12800]{1,0:T(8,128)} %get-tuple-element.13, f32[2048]{0:T(1024)S(1)} %get-tuple-element.12, s32[2048]{0:T(1024)S(1)} %bitcast.8), kind=kLoop, calls=%fused_computation.4 | loop fusion | flops 183494656 | bytes 104898560 | tf_op jit(solution)/shard_map/reduce_sum | solution.py:31
  734.6 1.7 gather_fusion.1
  736.3 26.0 %all-reduce = (f32[2048]{0:T(1024)S(1)}, f32[2048]{0:T(1024)S(1)}, f32[2048]{0:T(1024)S(1)}) all-reduce(f32[2048]{0:T(1024)S(1)} %get-tuple-element.4, f32[2048]{0:T(1024)S(1)} %get-tuple-element.9, f32[2048]{0:T(1024)S(1)} %get-tuple-element.8), channel_id=1, replica_groups=mesh['dp'=4,'tensor'=8] {'tensor'}, use_global_device_ids=true, to_apply=%region_3.0 | all-reduce | flops 6144 | bytes 49152 | tf_op jit(solution)/shard_map/psum | solution.py:45
  762.3 1.7 gather_fusion
  764.0 1.7 gather_fusion.2
  765.8 1.7 gather_fusion.3
  767.5 0.6 subtract_select_fusion
  (7 shorter events, 0.0 us)
Async XLA Ops:
  7.2 89.0 %all-gather.4.cloned.1.call-start = ((), (), s32[]{:S(2)}) async-start(), calls=%async_computation | async-start | bytes 9437184 | tf_op jit(solution)/shard_map/all_gather | solution.py:24
  11.3 540.9 %all-gather.6.cloned.1.call-start = ((), (), s32[]{:S(2)}) async-start(), calls=%async_computation.1 | async-start | bytes 65536000 | tf_op jit(solution)/shard_map/all_gather | solution.py:16
  552.2 139.0 %copy-start = (s32[1,8,256]{2,1,0:T(8,128)S(1)}, s32[1,8,256]{2,1,0:T(8,128)}, u32[]{:S(2)}) copy-start(s32[1,8,256]{2,1,0:T(8,128)} %broadcast_subtract_fusion) | copy-start | bytes 24580
  691.1 43.4 %copy-start.1 = (s32[1024]{0:T(1024)S(1)}, s32[1024]{0:T(1024)}, u32[]{:S(2)}) copy-start(s32[1024]{0:T(1024)} %pad_clamp_fusion) | copy-start | bytes 12292
  691.1 76.4 %copy-start.2 = (s32[256]{0:T(256)S(1)}, s32[256]{0:T(256)}, u32[]{:S(2)}) copy-start(s32[256]{0:T(256)} %select_reduce_fusion.1) | copy-start | bytes 3076
Sparse Core Ops, SparseCore 0:
  11.4 84.7 all-gather.3
  98.1 454.0 all-gather.5
where the time goes:
time: 775 us
  waiting for transfers between devices  525 us (68%)
  matrix products  122 us (16%)
  blocking collectives  56.4 us (7%)
  other arithmetic  50.6 us (7%)
  between operations  14.1 us (2%)
    all_gather x1, waiting for transfers between devices, per_device(): weight = lax.all_gather(head_weight, 'dp', axis=0, tiled=True)  456 us
    dot_general x1, matrix products, per_device(): jnp.dot(lax.all_gather(normed, 'tensor', axis=0, tiled=True), weight, pre...  122 us
    all_gather x1, waiting for transfers between devices, per_device(): lax.all_gather(normed, 'tensor', axis=0, tiled=True)  68 us
    reduce_sum x1, other arithmetic, per_device(): moment = jnp.sum(expo * logits, axis=1)  43.4 us
    psum x1, blocking collectives, per_device(): lax.psum((total * rescale, moment * rescale, chosen), 'tensor')  26 us
    pmax x1, blocking collectives, per_device(): top_all = lax.pmax(top, 'tensor')  16.8 us
  transfers between devices with their start and end apart: 2, of which 2 were waited for; matrix products, arithmetic and copies ran while one was open for 0% of the time, Pallas kernels for 0%

commit v1 on v0

v1 whole, which is shorter than its diff:
```python
import functools

import jax
import jax.numpy as jnp
from jax import lax
from jax.experimental import pallas as pl
from jax.experimental.pallas import tpu as pltpu
from jax.sharding import PartitionSpec as P

SEQ_DP = 4
SLOT = 512
MESH = pl.DeviceIdType.MESH
TAIL = 128


def normalize(hidden, norm_gain):
    wide = hidden.astype(jnp.float32)
    meansq = jnp.mean(wide * wide, axis=-1, keepdims=True)
    return (wide * lax.rsqrt(meansq + 1e-06) * norm_gain).astype(jnp.bfloat16)


def plain_device(hidden, norm_gain, head_weight, token_ids, lengths):
    row_dev = hidden.shape[0]
    tensor_idx = lax.axis_index("tensor")
    normed = normalize(hidden, norm_gain)
    weight = lax.all_gather(head_weight, "dp", axis=0, tiled=True)
    vocab_dev = weight.shape[1]
    own_rows = tensor_idx * row_dev + jnp.arange(row_dev, dtype=jnp.int32)
    logits = jnp.dot(
        lax.all_gather(normed, "tensor", axis=0, tiled=True),
        weight,
        preferred_element_type=jnp.float32,
    )
    top = jnp.max(logits, axis=1)
    expo = jnp.exp(logits - top[:, None])
    total = jnp.sum(expo, axis=1)
    moment = jnp.sum(expo * logits, axis=1)
    ids = lax.all_gather(token_ids, "tensor", axis=0, tiled=True) - tensor_idx * vocab_dev
    hit = ids[:, None] == jnp.arange(vocab_dev, dtype=jnp.int32)[None, :]
    chosen = jnp.sum(jnp.where(hit, logits, 0.0), axis=1)
    seq_iota = jnp.arange(SEQ_DP, dtype=jnp.int32)
    onehot = (own_rows // SLOT)[:, None] == seq_iota[None, :]
    length_of = jnp.sum(jnp.where(onehot, lengths[0][None, :], 0), axis=1)
    scored = own_rows % SLOT < length_of
    top_all = lax.pmax(top, "tensor")
    rescale = jnp.exp(top - top_all)
    total_all, moment_all, chosen_all = lax.psum(
        (total * rescale, moment * rescale, chosen), "tensor"
    )
    return finish(
        scored, top_all[own_rows], total_all[own_rows], moment_all[own_rows], chosen_all[own_rows]
    )


def finish(scored, top, total, moment, chosen):
    safe_total = jnp.where(scored, total, 1.0)
    lse = top + jnp.log(safe_total)
    logprob = jnp.where(scored, chosen - lse, 0.0)
    entropy = jnp.where(scored, lse - moment / safe_total, 0.0)
    return (logprob, entropy)


def head_kernel(
    n_dp, n_z, chunks, x_ref, w_ref, out_ref,
    rows, weight, buf_a, buf_b, acc,
    plane_send, plane_recv, up_send, up_recv, down_send, down_recv,
    sib_send, sib_recv, w_send, w_recv, local_sem,
):
    dp = lax.axis_index("dp")
    t = lax.axis_index("tensor")
    z, core = t // 2, t % 2
    depth = w_ref.shape[0]
    vocab = weight.shape[1]
    share = x_ref.shape[0]
    width = weight.shape[0]
    block = n_dp * share

    barrier = pltpu.get_barrier_semaphore()
    for k in range(1, n_dp):
        pl.semaphore_signal(barrier, device_id=((dp + k) % n_dp, t), device_id_type=MESH)
    pl.semaphore_signal(barrier, device_id=(dp, z * 2 + 1 - core), device_id_type=MESH)

    @pl.when(z > 0)
    def _():
        pl.semaphore_signal(barrier, device_id=(dp, t - 2), device_id_type=MESH)

    @pl.when(z < n_z - 1)
    def _():
        pl.semaphore_signal(barrier, device_id=(dp, t + 2), device_id_type=MESH)

    ends = (z == 0).astype(jnp.int32) + (z == n_z - 1).astype(jnp.int32)
    pl.semaphore_wait(barrier, n_dp + 2 - ends)

    def remote(src, dst, send, recv, to):
        return pltpu.make_async_remote_copy(
            src_ref=src, dst_ref=dst, send_sem=send, recv_sem=recv,
            device_id=to, device_id_type=MESH,
        )

    def plane_copy(k, sender):
        return remote(
            x_ref,
            rows.at[z, core, pl.ds(pl.multiple_of(sender * share, share), share)],
            plane_send.at[k - 1], plane_recv.at[k - 1], ((dp + k) % n_dp, t),
        )

    for k in range(1, n_dp):
        plane_copy(k, dp).start()
    own_rows = pltpu.make_async_copy(
        x_ref, rows.at[z, core, pl.ds(pl.multiple_of(dp * share, share), share)], local_sem.at[0]
    )
    own_rows.start()

    def weight_copy(k, sender):
        peer = (dp + k) % n_dp
        return remote(
            w_ref.at[:, pl.ds(pl.multiple_of(peer * vocab, 128), vocab)],
            weight.at[pl.ds(pl.multiple_of(sender * depth, depth), depth)],
            w_send.at[k - 1], w_recv.at[k - 1], (peer, t),
        )

    for k in range(1, n_dp):
        weight_copy(k, dp).start()
    own_weight = pltpu.make_async_copy(
        w_ref.at[:, pl.ds(pl.multiple_of(dp * vocab, 128), vocab)],
        weight.at[pl.ds(pl.multiple_of(dp * depth, depth), depth)],
        local_sem.at[1],
    )
    own_weight.start()

    def up_copy(d):
        plane = z - d
        return remote(
            rows.at[plane, core], rows.at[plane, core],
            up_send.at[d], up_recv.at[d], (dp, t + 2),
        )

    def down_copy(d):
        plane = z + d
        return remote(
            rows.at[plane, core], rows.at[plane, core],
            down_send.at[d], down_recv.at[d], (dp, t - 2),
        )

    def sib_copy(plane, half):
        return remote(
            rows.at[plane, half], rows.at[plane, half],
            sib_send.at[plane], sib_recv.at[plane], (dp, z * 2 + 1 - core),
        )

    for k in range(1, n_dp):
        plane_copy(k, (dp - k + n_dp) % n_dp).wait_recv()
    own_rows.wait()

    @pl.when(z < n_z - 1)
    def _():
        up_copy(0).start()

    @pl.when(z > 0)
    def _():
        down_copy(0).start()

    sib_copy(z, core).start()

    for d in range(1, n_z):
        @pl.when(z >= d)
        def _():
            remote(
                rows.at[z - d, core], rows.at[z - d, core],
                up_send.at[d - 1], up_recv.at[d - 1], (dp, t),
            ).wait_recv()

            @pl.when(z < n_z - 1)
            def _():
                up_copy(d).start()

            sib_copy(z - d, core).start()

        @pl.when(z + d < n_z)
        def _():
            remote(
                rows.at[z + d, core], rows.at[z + d, core],
                down_send.at[d - 1], down_recv.at[d - 1], (dp, t),
            ).wait_recv()

            @pl.when(z > 0)
            def _():
                down_copy(d).start()

            sib_copy(z + d, core).start()

    for plane in range(n_z):
        sib_copy(plane, 1 - core).wait_recv()
    for k in range(1, n_dp):
        weight_copy(k, (dp - k + n_dp) % n_dp).wait_recv()
    own_weight.wait()

    first = t * (n_dp * vocab) + dp * vocab
    lane = lax.broadcasted_iota(jnp.int32, (1, 128), 1)
    strip = 16

    @pl.loop(0, n_z * 2)
    def _(step):
        plane, half = step // 2, step % 2
        tail = rows[plane, half, :, width:].astype(jnp.float32)
        place = jnp.where(
            lane == 0, 4096.0, jnp.where(lane == 1, 64.0, jnp.where(lane == 2, 1.0, 0.0))
        )
        ids = jnp.sum(tail * place, axis=1, keepdims=True).astype(jnp.int32)
        acc[0] = jnp.full((block, 128), -3e38, jnp.float32)
        acc[1] = jnp.zeros((block, 128), jnp.float32)
        acc[2] = jnp.zeros((block, 128), jnp.float32)
        acc[3] = jnp.zeros((block, 128), jnp.float32)
        shifted = ids - first - lane
        lhs = rows[plane, half, :, :width]
        at = 0
        for i, size in enumerate(chunks):
            buf = (buf_a, buf_b)[i % 2]
            buf[:, :size] = jnp.dot(
                lhs, weight[:, at : at + size], preferred_element_type=jnp.float32
            )
            for r in range(0, block, strip):
                part = slice(r, r + strip)
                groups = [buf[part, g : g + 128] for g in range(0, size, 128)]
                old = acc[0, part]
                top = old
                for g in groups:
                    top = jnp.maximum(top, g)
                scale = jnp.exp(old - top)
                total = acc[1, part] * scale
                moment = acc[2, part] * scale
                chosen = acc[3, part]
                for n, g in enumerate(groups):
                    e = jnp.exp(g - top)
                    total += e
                    moment += e * g
                    chosen += jnp.where(shifted[part] == at + n * 128, g, 0.0)
                acc[0, part] = top
                acc[1, part] = total
                acc[2, part] = moment
                acc[3, part] = chosen
            at += size
        top = jnp.max(acc[0], axis=1, keepdims=True)
        scale = jnp.exp(acc[0] - top)
        total = jnp.sum(acc[1] * scale, axis=1, keepdims=True)
        moment = jnp.sum(acc[2] * scale, axis=1, keepdims=True)
        chosen = jnp.sum(acc[3], axis=1, keepdims=True)
        packed = jnp.where(
            lane == 0, top, jnp.where(lane == 1, total, jnp.where(lane == 2, moment, chosen))
        )
        out_ref[step] = packed.T[:8]

    for k in range(1, n_dp):
        plane_copy(k, dp).wait_send()
        weight_copy(k, dp).wait_send()
    for plane in range(n_z):
        sib_copy(plane, core).wait_send()
    for d in range(n_z - 1):
        @pl.when((z >= d) & (z < n_z - 1))
        def _():
            up_copy(d).wait_send()

        @pl.when((z + d < n_z) & (z > 0))
        def _():
            down_copy(d).wait_send()


def head_stats(n_dp, n_z, mine, head_weight):
    share, wide = mine.shape
    depth, vocab_dev = head_weight.shape
    width, vocab, block = n_dp * depth, vocab_dev // n_dp, n_dp * share
    chunks = [512] * (vocab // 512) + ([vocab % 512] if vocab % 512 else [])
    dma = pltpu.SemaphoreType.DMA
    flops = 2 * n_z * 2 * block * width * vocab
    return pl.pallas_call(
        functools.partial(head_kernel, n_dp, n_z, chunks),
        out_shape=jax.ShapeDtypeStruct((n_z * 2, 8, block), jnp.float32),
        in_specs=[
            pl.BlockSpec(memory_space=pltpu.VMEM),
            pl.BlockSpec(memory_space=pl.ANY),
        ],
        out_specs=pl.BlockSpec(memory_space=pltpu.VMEM),
        scratch_shapes=[
            pltpu.VMEM((n_z, 2, block, wide), jnp.bfloat16),
            pltpu.VMEM((width, vocab), jnp.bfloat16),
            pltpu.VMEM((block, 512), jnp.float32),
            pltpu.VMEM((block, 512), jnp.float32),
            pltpu.VMEM((4, block, 128), jnp.float32),
            dma((n_dp - 1,)), dma((n_dp - 1,)),
            dma((n_z,)), dma((n_z,)), dma((n_z,)), dma((n_z,)),
            dma((n_z,)), dma((n_z,)),
            dma((n_dp - 1,)), dma((n_dp - 1,)),
            dma((2,)),
        ],
        compiler_params=pltpu.CompilerParams(
            collective_id=0, has_side_effects=True, vmem_limit_bytes=56 * 1024 * 1024
        ),
        cost_estimate=pl.CostEstimate(
            flops=flops, bytes_accessed=width * vocab * 2, transcendentals=n_z * 2 * block * vocab
        ),
    )(mine, head_weight)


def last_at_or_below(starts, value):
    return jnp.sum((value[:, None] >= starts[None, :]).astype(jnp.int32), axis=1) - 1


def pick(table, index):
    iota = jnp.arange(table.shape[0], dtype=jnp.int32)
    return jnp.sum(jnp.where(index[:, None] == iota[None, :], table[None, :], 0), axis=1)


def kernel_device(n_dp, n_tensor, hidden, norm_gain, head_weight, token_ids, lengths):
    row_dev = hidden.shape[0]
    n_z = n_tensor // 2
    t = lax.axis_index("tensor")
    z, core = t // 2, t % 2
    length = lengths[0]
    over = jnp.maximum(length - row_dev, 0)
    under = jnp.maximum(row_dev - length, 0)
    over_at = jnp.cumsum(over) - over
    under_at = jnp.cumsum(under) - under

    normed = normalize(hidden, norm_gain)
    lane = jnp.arange(TAIL, dtype=jnp.int32)[None, :]
    ids = token_ids[:, None]
    digits = jnp.where(
        lane == 0, ids // 4096, jnp.where(lane == 1, ids // 64 % 64, jnp.where(lane == 2, ids % 64, 0))
    )
    sent = jnp.concatenate([normed, digits.astype(jnp.bfloat16)], axis=1)

    share = row_dev // 2
    slot = t * share + jnp.arange(share, dtype=jnp.int32)
    place = slot % row_dev
    zs = jnp.full((share,), z, jnp.int32)
    own_len = pick(length, zs)
    extra = pick(under_at, zs) + place - own_len
    giver = last_at_or_below(over_at, extra)
    source = jnp.where(
        place < own_len,
        z * SLOT + place,
        giver * SLOT + row_dev + extra - pick(over_at, giver),
    )
    everyone = lax.all_gather(sent, "tensor", axis=0, tiled=True)
    chooser = source[:, None] == jnp.arange(n_tensor * row_dev, dtype=jnp.int32)[None, :]
    mine = jnp.dot(
        chooser.astype(jnp.bfloat16), everyone, preferred_element_type=jnp.float32
    ).astype(jnp.bfloat16)

    stats = head_stats(n_dp, n_z, mine, head_weight)[:, :4]
    stats = stats.reshape(n_tensor, 4, n_dp, share).transpose(2, 1, 0, 3).reshape(n_dp, 4, -1)

    def merge(parts):
        top = jnp.max(parts[:, 0], axis=0)
        scale = jnp.exp(parts[:, 0] - top)
        return jnp.stack([
            top,
            jnp.sum(parts[:, 1] * scale, axis=0),
            jnp.sum(parts[:, 2] * scale, axis=0),
            jnp.sum(parts[:, 3], axis=0),
        ])

    part = merge(lax.all_to_all(stats, "dp", 0, 0))
    full = merge(lax.all_gather(part, "tensor", axis=0))

    row = jnp.arange(row_dev, dtype=jnp.int32)
    zr = jnp.full((row_dev,), z, jnp.int32)
    extra = pick(over_at, zr) + row
    taker = last_at_or_below(under_at, extra)
    back = taker * row_dev + pick(length, taker) + extra - pick(under_at, taker)
    where = jnp.where(core == 0, z * row_dev + row, back)
    scored = core * row_dev + row < pick(length, zr)
    hit = where[:, None] == jnp.arange(n_tensor * share, dtype=jnp.int32)[None, :]
    own = [jnp.sum(jnp.where(hit, full[i][None, :], 0.0), axis=1) for i in range(4)]
    return finish(scored, *own)


def solution(mesh):
    n_dp, n_tensor = mesh.shape["dp"], mesh.shape["tensor"]

    def per_device(hidden, norm_gain, head_weight, token_ids, lengths):
        fits = (
            n_tensor == 2 * SEQ_DP
            and 2 * hidden.shape[0] == SLOT
            and head_weight.shape[1] % (128 * n_dp) == 0
        )
        if not fits:
            return plain_device(hidden, norm_gain, head_weight, token_ids, lengths)
        return kernel_device(n_dp, n_tensor, hidden, norm_gain, head_weight, token_ids, lengths)

    return jax.shard_map(
        per_device,
        mesh=mesh,
        in_specs=(
            P(("dp", "tensor"), None),
            P(),
            P("dp", "tensor"),
            P(("dp", "tensor")),
            P("dp", None),
        ),
        out_specs=(P(("dp", "tensor")), P(("dp", "tensor"))),
        check_vma=False,
    )
```

time: 775 us -> 384 us (0.50)
  waiting for transfers between devices: 525 us -> 93.1 us
  Pallas kernels: 0 us -> 244 us
  matrix products: 122 us -> 5.84 us
  other arithmetic: 50.6 us -> 7.61 us
  blocking collectives: 56.4 us -> 14 us
    all_gather x2 -> x1, waiting for transfers between devices: 524 us -> 88.3 us  [kernel_device(): everyone = lax.all_gather(sent, 'tensor', axis=0, tiled=True)]
    pallas_call x0 -> x1, Pallas kernels: none -> 244 us  [head_stats(): pl.pallas_call(functools.partial(head_kernel, n_dp, n_z, chunks), out_sha...]
    dot_general x1, matrix products: 122 us -> 5.84 us  [kernel_device(): jnp.dot(chooser.astype(jnp.bfloat16), everyone, preferred_element_type=jn...]
    reduce_sum x3 -> x10, other arithmetic: 46.2 us -> 2.8 us  [the longest x1 1.51 us: normalize(): meansq = jnp.mean(wide * wide, axis=-1, keepdims=True)]
    psum x1 -> x0, blocking collectives: 26 us -> none  [per_device(): lax.psum((total * rescale, moment * rescale, chosen), 'tensor')]
    pmax x1 -> x0, blocking collectives: 16.8 us -> none  [per_device(): top_all = lax.pmax(top, 'tensor')]
where the time goes in v1:
time: 384 us; the launch traced here: 383 us
  Pallas kernels  244 us (64%)
  waiting for transfers between devices  93.1 us (24%)
  between operations  14.2 us (4%)
  blocking collectives  14 us (4%)
  other arithmetic  7.61 us (2%)
  matrix products  5.84 us (2%)
    pallas_call x1, Pallas kernels, head_stats(): pl.pallas_call(functools.partial(head_kernel, n_dp, n_z, chunks), out_sha...  244 us
    all_gather x1, waiting for transfers between devices, kernel_device(): everyone = lax.all_gather(sent, 'tensor', axis=0, tiled=True)  88.3 us
    all_gather x1, blocking collectives, kernel_device(): full = merge(lax.all_gather(part, 'tensor', axis=0))  14 us
  transfers between devices with their start and end apart: 2, of which 2 were waited for; matrix products, arithmetic and copies ran while one was open for 0% of the time, Pallas kernels for 0%

profile of v1, /device:TPU:0, one launch (start us, length us, event | category | flops | bytes accessed | tf_op | source)
XLA Modules:
  0.0 383.2 jit_solution(2689143817770761364)
XLA Ops:
  7.2 0.7 and_select_fusion.3
  7.9 1.5 fusion
  9.5 1.5 fusion.2
  11.0 0.2 select_convert_fusion
  11.2 1.2 pad_maximum_fusion
  12.4 0.2 reduce-window_clone.1
  12.6 0.2 reduce-window_1_clone.1
  12.8 0.1 select_reduce_fusion.9
  12.9 0.1 convert_reduce_fusion.1
  13.0 0.1 select_reduce_fusion.8
  13.1 0.1 select_reduce_fusion.7
  13.2 0.1 convert_reduce_fusion
  13.2 0.1 select_reduce_fusion.5
  13.4 88.3 %all-gather.4.cloned.1.call-done = bf16[2048,2176]{1,0:T(8,128)(2,1)} async-done(((bf16[256,2176]{1,0:T(8,128)(2,1)}), bf16[2048,2176]{1,0:T(8,128)(2,1)}) %all-gather.4.cloned.1.call-update) | async-done | bytes 8912912 | tf_op jit(solution)/shard_map/all_gather | solution.py:344
  101.6 5.8 %convolution_convert_fusion.x_ref = bf16[128,2176]{1,0:T(8,128)(2,1)} fusion(bf16[2048,2176]{1,0:T(8,128)(2,1)} %all-gather.4.cloned.1.call-done, s32[128]{0:T(128)S(1)} %compare_select_fusion.4), kind=kOutput, calls=%fused_computation | convolution fusion | flops 1141391360 | bytes 9470464 | tf_op jit(solution)/shard_map/dot_general | solution.py:346
  107.5 243.5 %shard_map.68 = f32[8,8,512]{2,1,0:T(8,128)} custom-call(bf16[128,2176]{1,0:T(8,128)(2,1)} %convolution_convert_fusion.x_ref, bf16[512,12800]{1,0:T(8,128)(2,1)} %w_ref.1), custom_call_target="tpu_custom_call" | custom-call | flops 53687091200 | bytes 13107200 | tf_op jit(solution)/shard_map/pallas_call | solution.py:275
  351.0 0.9 slice.29
  352.0 0.6 reshape.176
  352.6 3.3 all-to-all-start
  355.9 4.9 %all-to-all-done = f32[4,4,1024]{2,1,0:T(4,128)S(1)} async-done(((f32[4,4,1024]{2,1,0:T(4,128)}), f32[4,4,1024]{2,1,0:T(4,128)S(1)}, u32[]{:S(2)}, u32[]{:S(2)}) %all-to-all-start) | async-done | bytes 65568 | tf_op jit(solution)/shard_map/all_to_all | solution.py:363
  360.9 14.0 %all-gather.1 = f32[8,4,1024]{2,1,0:T(4,128)S(1)} all-gather(f32[1,4,1024]{2,1,0:T(4,128)S(1)} %maximum_bitcast_fusion), channel_id=2, replica_groups=mesh['dp'=4,'tensor'=8] {'tensor'}, dimensions={0}, use_global_device_ids=true | all-gather | bytes 147456 | tf_op jit(solution)/shard_map/all_gather | solution.py:364
  374.9 0.1 fusion.16
  375.1 0.7 select_reduce_fusion
  375.8 0.6 subtract_select_fusion
  (22 shorter events, 0.4 us)
Async XLA Ops:
  7.2 94.5 %all-gather.4.cloned.1.call-start = ((), (), s32[]{:S(2)}) async-start(), calls=%async_computation.1 | async-start | bytes 10027008 | tf_op jit(solution)/shard_map/all_gather | solution.py:344
  11.0 1.4 copy-start
  352.6 8.2 %all-to-all-start = ((f32[4,4,1024]{2,1,0:T(4,128)}), f32[4,4,1024]{2,1,0:T(4,128)S(1)}, u32[]{:S(2)}, u32[]{:S(2)}) async-start(f32[4,4,1024]{2,1,0:T(4,128)} %reshape.176), calls=%async_computation | async-start | bytes 131072 | tf_op jit(solution)/shard_map/all_to_all | solution.py:363
Sparse Core Ops, SparseCore 0:
  12.5 89.0 all-gather.3

commit v2 on v1

v2 whole, which is shorter than its diff:
```python
import functools

import jax
import jax.numpy as jnp
from jax import lax
from jax.experimental import pallas as pl
from jax.experimental.pallas import tpu as pltpu
from jax.sharding import PartitionSpec as P

SEQ_DP = 4
SLOT = 512
MESH = pl.DeviceIdType.MESH
TAIL = 128


def normalize(hidden, norm_gain):
    wide = hidden.astype(jnp.float32)
    meansq = jnp.mean(wide * wide, axis=-1, keepdims=True)
    return (wide * lax.rsqrt(meansq + 1e-06) * norm_gain).astype(jnp.bfloat16)


def plain_device(hidden, norm_gain, head_weight, token_ids, lengths):
    row_dev = hidden.shape[0]
    tensor_idx = lax.axis_index("tensor")
    normed = normalize(hidden, norm_gain)
    weight = lax.all_gather(head_weight, "dp", axis=0, tiled=True)
    vocab_dev = weight.shape[1]
    own_rows = tensor_idx * row_dev + jnp.arange(row_dev, dtype=jnp.int32)
    logits = jnp.dot(
        lax.all_gather(normed, "tensor", axis=0, tiled=True),
        weight,
        preferred_element_type=jnp.float32,
    )
    top = jnp.max(logits, axis=1)
    expo = jnp.exp(logits - top[:, None])
    total = jnp.sum(expo, axis=1)
    moment = jnp.sum(expo * logits, axis=1)
    ids = lax.all_gather(token_ids, "tensor", axis=0, tiled=True) - tensor_idx * vocab_dev
    hit = ids[:, None] == jnp.arange(vocab_dev, dtype=jnp.int32)[None, :]
    chosen = jnp.sum(jnp.where(hit, logits, 0.0), axis=1)
    seq_iota = jnp.arange(SEQ_DP, dtype=jnp.int32)
    onehot = (own_rows // SLOT)[:, None] == seq_iota[None, :]
    length_of = jnp.sum(jnp.where(onehot, lengths[0][None, :], 0), axis=1)
    scored = own_rows % SLOT < length_of
    top_all = lax.pmax(top, "tensor")
    rescale = jnp.exp(top - top_all)
    total_all, moment_all, chosen_all = lax.psum(
        (total * rescale, moment * rescale, chosen), "tensor"
    )
    return finish(
        scored, top_all[own_rows], total_all[own_rows], moment_all[own_rows], chosen_all[own_rows]
    )


def finish(scored, top, total, moment, chosen):
    safe_total = jnp.where(scored, total, 1.0)
    lse = top + jnp.log(safe_total)
    logprob = jnp.where(scored, chosen - lse, 0.0)
    entropy = jnp.where(scored, lse - moment / safe_total, 0.0)
    return (logprob, entropy)


def head_kernel(
    n_dp, n_z, groups, x_ref, sel_ref, keep_ref, w_ref, out_ref,
    rows, weight, back, front, buf_a, buf_b, acc, stats, dp_parts, part, all_parts,
    plane_send, plane_recv, up_send, up_recv, down_send, down_recv,
    sib_send, sib_recv, w_send, w_recv, local_sem,
    bup_send, bup_recv, bdown_send, bdown_recv, bsib_send, bsib_recv,
    front_send, front_recv, sdp_send, sdp_recv, st_send, st_recv,
):
    dp = lax.axis_index("dp")
    t = lax.axis_index("tensor")
    z, core = t // 2, t % 2
    n_tensor = 2 * n_z
    depth = w_ref.shape[0]
    width, vocab = weight.shape
    share, wide = front.shape
    block = n_dp * share
    sibling = (dp, z * 2 + 1 - core)
    above, below = (dp, t + 2), (dp, t - 2)

    barrier = pltpu.get_barrier_semaphore()
    for k in range(1, n_dp):
        pl.semaphore_signal(barrier, device_id=((dp + k) % n_dp, t), device_id_type=MESH)
    for k in range(1, n_tensor):
        pl.semaphore_signal(barrier, device_id=(dp, (t + k) % n_tensor), device_id_type=MESH)
    pl.semaphore_wait(barrier, n_dp + n_tensor - 2)

    def remote(src, dst, send, recv, to):
        return pltpu.make_async_remote_copy(
            src_ref=src, dst_ref=dst, send_sem=send, recv_sem=recv,
            device_id=to, device_id_type=MESH,
        )

    def back_up(d):
        src = x_ref if d == 0 else back.at[z - d]
        return remote(src, back.at[z - d], bup_send.at[d], bup_recv.at[d], above)

    def back_down(d):
        src = x_ref if d == 0 else back.at[z + d]
        return remote(src, back.at[z + d], bdown_send.at[d], bdown_recv.at[d], below)

    def back_sib(plane):
        return remote(
            back.at[plane], back.at[plane], bsib_send.at[plane], bsib_recv.at[plane], sibling
        )

    front_copy = remote(x_ref.at[share : 2 * share], front, front_send, front_recv, sibling)
    own_front = pltpu.make_async_copy(x_ref.at[0:share], front, local_sem.at[0])

    @pl.when((core == 1) & (z < n_z - 1))
    def _():
        back_up(0).start()

    @pl.when((core == 1) & (z > 0))
    def _():
        back_down(0).start()

    @pl.when(core == 0)
    def _():
        front_copy.start()
        own_front.start()

    def weight_copy(g, k, sender):
        at, size = groups[g][0], sum(groups[g][1])
        peer = (dp + k) % n_dp
        return remote(
            w_ref.at[:, pl.ds(pl.multiple_of(peer * vocab + at, 128), size)],
            weight.at[pl.ds(pl.multiple_of(sender * depth, depth), depth), at : at + size],
            w_send.at[g, k - 1], w_recv.at[g, k - 1], (peer, t),
        )

    for g in range(2):
        for k in range(1, n_dp):
            weight_copy(g, k, dp).start()
    own_weight = pltpu.make_async_copy(
        w_ref.at[:, pl.ds(pl.multiple_of(dp * vocab, 128), vocab)],
        weight.at[pl.ds(pl.multiple_of(dp * depth, depth), depth)],
        local_sem.at[1],
    )
    own_weight.start()

    for d in range(1, n_z):
        @pl.when((core == 1) & (z >= d))
        def _():
            remote(
                back.at[z - d], back.at[z - d], bup_send.at[d - 1], bup_recv.at[d - 1], above
            ).wait_recv()

            @pl.when(z < n_z - 1)
            def _():
                back_up(d).start()

            back_sib(z - d).start()

        @pl.when((core == 1) & (z + d < n_z))
        def _():
            remote(
                back.at[z + d], back.at[z + d], bdown_send.at[d - 1], bdown_recv.at[d - 1], below
            ).wait_recv()

            @pl.when(z > 0)
            def _():
                back_down(d).start()

            back_sib(z + d).start()

    @pl.when(core == 0)
    def _():
        own_front.wait()
        for k in range(1, n_z):
            back_sib((z + k) % n_z).wait_recv()

    @pl.when(core == 1)
    def _():
        front_copy.wait_recv()

    own_at = pl.ds(pl.multiple_of(dp * share, share), share)
    for at in range(0, wide, 512):
        cols = slice(at, min(at + 512, wide))
        mine = front[:, cols].astype(jnp.float32) * keep_ref[:, :1]
        for k in range(1, n_z):
            plane = (z + k) % n_z
            mine += jnp.dot(
                sel_ref[plane], back[plane, :, cols], preferred_element_type=jnp.float32
            )
        rows[z, core, own_at, cols] = mine.astype(jnp.bfloat16)

    def plane_copy(k, sender):
        at = pl.ds(pl.multiple_of(sender * share, share), share)
        return remote(
            rows.at[z, core, at], rows.at[z, core, at],
            plane_send.at[k - 1], plane_recv.at[k - 1], ((dp + k) % n_dp, t),
        )

    for k in range(1, n_dp):
        plane_copy(k, dp).start()

    def up_copy(d):
        ref = rows.at[z - d, core]
        return remote(ref, ref, up_send.at[d], up_recv.at[d], above)

    def down_copy(d):
        ref = rows.at[z + d, core]
        return remote(ref, ref, down_send.at[d], down_recv.at[d], below)

    def sib_copy(plane, half):
        ref = rows.at[plane, half]
        return remote(ref, ref, sib_send.at[plane], sib_recv.at[plane], sibling)

    for k in range(1, n_dp):
        plane_copy(k, (dp - k + n_dp) % n_dp).wait_recv()

    @pl.when(z < n_z - 1)
    def _():
        up_copy(0).start()

    @pl.when(z > 0)
    def _():
        down_copy(0).start()

    sib_copy(z, core).start()

    def stage(d):
        @pl.when(z >= d)
        def _():
            ref = rows.at[z - d, core]
            remote(ref, ref, up_send.at[d - 1], up_recv.at[d - 1], above).wait_recv()

            @pl.when(z < n_z - 1)
            def _():
                up_copy(d).start()

            sib_copy(z - d, core).start()

        @pl.when(z + d < n_z)
        def _():
            ref = rows.at[z + d, core]
            remote(ref, ref, down_send.at[d - 1], down_recv.at[d - 1], below).wait_recv()

            @pl.when(z > 0)
            def _():
                down_copy(d).start()

            sib_copy(z + d, core).start()

    def wait_weights(g):
        for k in range(1, n_dp):
            weight_copy(g, k, (dp - k + n_dp) % n_dp).wait_recv()

    stage(1)
    own_weight.wait()
    wait_weights(0)

    first = t * (n_dp * vocab) + dp * vocab
    lane = lax.broadcasted_iota(jnp.int32, (1, 128), 1)
    strip = 16

    def multiply(plane, half, g):
        entry = plane * 2 + half
        tail = rows[plane, half, :, width:].astype(jnp.float32)
        place = jnp.where(
            lane == 0, 4096.0, jnp.where(lane == 1, 64.0, jnp.where(lane == 2, 1.0, 0.0))
        )
        ids = jnp.sum(tail * place, axis=1, keepdims=True).astype(jnp.int32)
        shifted = ids - first - lane
        lhs = rows[plane, half, :, :width]
        at, sizes = groups[g]
        for i, size in enumerate(sizes):
            buf = (buf_a, buf_b)[i % 2]
            buf[:, :size] = jnp.dot(
                lhs, weight[:, at : at + size], preferred_element_type=jnp.float32
            )
            for r in range(0, block, strip):
                rs = slice(r, r + strip)
                tiles = [buf[rs, c : c + 128] for c in range(0, size, 128)]
                old = acc[entry, 0, rs]
                top = old
                for tile in tiles:
                    top = jnp.maximum(top, tile)
                scale = jnp.exp(old - top)
                total = acc[entry, 1, rs] * scale
                moment = acc[entry, 2, rs] * scale
                chosen = acc[entry, 3, rs]
                for n, tile in enumerate(tiles):
                    e = jnp.exp(tile - top)
                    total += e
                    moment += e * tile
                    chosen += jnp.where(shifted[rs] == at + n * 128, tile, 0.0)
                acc[entry, 0, rs] = top
                acc[entry, 1, rs] = total
                acc[entry, 2, rs] = moment
                acc[entry, 3, rs] = chosen
            at += size

    near = n_z - 1

    @pl.loop(0, 4 * n_z)
    def _(it):
        unit, turn = it // 2, it % 2
        half = (core + turn) % 2
        second = ((unit >= near) & (unit < 2 * near)) | (unit == 2 * n_z - 1)
        order = jnp.where(unit < near, unit, jnp.where(unit < 2 * near, unit - near, near))
        plane = jnp.where(z < n_z // 2, order, n_z - 1 - order)
        entry = plane * 2 + half

        @pl.when(it == 4)
        def _():
            stage(2)

        @pl.when(it == 2 * near)
        def _():
            wait_weights(1)

        @pl.when(it == 4 * near)
        def _():
            stage(3)

        @pl.when(jnp.logical_not(second))
        def _():
            @pl.when(turn == 1)
            def _():
                sib_copy(plane, 1 - core).wait_recv()

            acc[entry, 0] = jnp.full((block, 128), -3e38, jnp.float32)
            for i in range(1, 4):
                acc[entry, i] = jnp.zeros((block, 128), jnp.float32)
            multiply(plane, half, 0)

        @pl.when(second)
        def _():
            multiply(plane, half, 1)
            lanes = acc[entry, 0]
            top = jnp.max(lanes, axis=1, keepdims=True)
            scale = jnp.exp(lanes - top)
            total = jnp.sum(acc[entry, 1] * scale, axis=1, keepdims=True)
            moment = jnp.sum(acc[entry, 2] * scale, axis=1, keepdims=True)
            chosen = jnp.sum(acc[entry, 3], axis=1, keepdims=True)
            packed = jnp.where(
                lane == 0, top, jnp.where(lane == 1, total, jnp.where(lane == 2, moment, chosen))
            )
            stats[entry] = packed.T[:8]

    def merge(parts, n):
        each = [parts[i] for i in range(n)]
        top = each[0][:, 0:1]
        for p in each[1:]:
            top = jnp.maximum(top, p[:, 0:1])
        total = moment = chosen = jnp.zeros_like(top)
        for p in each:
            scale = jnp.exp(p[:, 0:1] - top)
            total += p[:, 1:2] * scale
            moment += p[:, 2:3] * scale
            chosen += p[:, 3:4]
        return jnp.concatenate([top, total, moment, chosen] * 2, axis=1)

    def stats_dp(k, sender):
        peer = (dp + k) % n_dp
        return remote(
            stats.at[:, :, pl.ds(pl.multiple_of(peer * share, share), share)], dp_parts.at[sender],
            sdp_send.at[k - 1], sdp_recv.at[k - 1], (peer, t),
        )

    for k in range(1, n_dp):
        stats_dp(k, dp).start()
    own_stats = pltpu.make_async_copy(
        stats.at[:, :, pl.ds(pl.multiple_of(dp * share, share), share)], dp_parts.at[dp], local_sem.at[2]
    )
    own_stats.start()
    own_stats.wait()
    for k in range(1, n_dp):
        stats_dp(k, (dp - k + n_dp) % n_dp).wait_recv()
    part[...] = merge(dp_parts, n_dp)

    def stats_t(k, sender):
        return remote(
            part, all_parts.at[sender], st_send.at[k - 1], st_recv.at[k - 1],
            (dp, (t + k) % n_tensor),
        )

    for k in range(1, n_tensor):
        stats_t(k, t).start()
    all_parts[t] = part[...]
    for k in range(1, n_tensor):
        stats_t(k, (t - k + n_tensor) % n_tensor).wait_recv()
    out_ref[...] = merge(all_parts, n_tensor)

    for k in range(1, n_dp):
        plane_copy(k, dp).wait_send()
        stats_dp(k, dp).wait_send()
        for g in range(2):
            weight_copy(g, k, dp).wait_send()
    for k in range(1, n_tensor):
        stats_t(k, t).wait_send()
    for plane in range(n_z):
        sib_copy(plane, core).wait_send()

    @pl.when(core == 0)
    def _():
        front_copy.wait_send()

    @pl.when(core == 1)
    def _():
        for k in range(1, n_z):
            back_sib((z + k) % n_z).wait_send()

    for d in range(n_z - 1):
        @pl.when((z >= d) & (z < n_z - 1))
        def _():
            up_copy(d).wait_send()

            @pl.when(core == 1)
            def _():
                back_up(d).wait_send()

        @pl.when((z + d < n_z) & (z > 0))
        def _():
            down_copy(d).wait_send()

            @pl.when(core == 1)
            def _():
                back_down(d).wait_send()


def head_stats(n_dp, n_z, sent, select, keep, head_weight):
    wide = sent.shape[1]
    share = sent.shape[0] // 2
    depth, vocab_dev = head_weight.shape
    width, vocab, block = n_dp * depth, vocab_dev // n_dp, n_dp * share
    sizes = [512] * (vocab // 512) + ([vocab % 512] if vocab % 512 else [])
    cut = len(sizes) // 2
    groups = [(0, sizes[:cut]), (sum(sizes[:cut]), sizes[cut:])]
    dma = pltpu.SemaphoreType.DMA
    n_tensor = 2 * n_z
    f32, bf16 = jnp.float32, jnp.bfloat16
    vmem = pl.BlockSpec(memory_space=pltpu.VMEM)
    return pl.pallas_call(
        functools.partial(head_kernel, n_dp, n_z, groups),
        out_shape=jax.ShapeDtypeStruct((n_tensor, 8, share), f32),
        in_specs=[vmem, vmem, vmem, pl.BlockSpec(memory_space=pl.ANY)],
        out_specs=vmem,
        scratch_shapes=[
            pltpu.VMEM((n_z, 2, block, wide), bf16),
            pltpu.VMEM((width, vocab), bf16),
            pltpu.VMEM((n_z, 2 * share, wide), bf16),
            pltpu.VMEM((share, wide), bf16),
            pltpu.VMEM((block, 512), f32),
            pltpu.VMEM((block, 512), f32),
            pltpu.VMEM((n_tensor, 4, block, 128), f32),
            pltpu.VMEM((n_tensor, 8, block), f32),
            pltpu.VMEM((n_dp, n_tensor, 8, share), f32),
            pltpu.VMEM((n_tensor, 8, share), f32),
            pltpu.VMEM((n_tensor, n_tensor, 8, share), f32),
            dma((n_dp - 1,)), dma((n_dp - 1,)),
            dma((n_z,)), dma((n_z,)), dma((n_z,)), dma((n_z,)),
            dma((n_z,)), dma((n_z,)),
            dma((2, n_dp - 1)), dma((2, n_dp - 1)),
            dma((3,)),
            dma((n_z,)), dma((n_z,)), dma((n_z,)), dma((n_z,)),
            dma((n_z,)), dma((n_z,)),
            dma, dma,
            dma((n_dp - 1,)), dma((n_dp - 1,)),
            dma((n_tensor - 1,)), dma((n_tensor - 1,)),
        ],
        compiler_params=pltpu.CompilerParams(
            collective_id=0, has_side_effects=True, vmem_limit_bytes=60 * 1024 * 1024
        ),
        cost_estimate=pl.CostEstimate(
            flops=2 * n_tensor * block * width * vocab,
            bytes_accessed=width * vocab * 2,
            transcendentals=n_tensor * block * vocab,
        ),
    )(sent, select, keep, head_weight)


def last_at_or_below(starts, value):
    return jnp.sum((value[:, None] >= starts[None, :]).astype(jnp.int32), axis=1) - 1


def pick(table, index):
    iota = jnp.arange(table.shape[0], dtype=jnp.int32)
    return jnp.sum(jnp.where(index[:, None] == iota[None, :], table[None, :], 0), axis=1)


def kernel_device(n_dp, n_tensor, hidden, norm_gain, head_weight, token_ids, lengths):
    row_dev = hidden.shape[0]
    n_z = n_tensor // 2
    t = lax.axis_index("tensor")
    z, core = t // 2, t % 2
    length = lengths[0]
    over = jnp.maximum(length - row_dev, 0)
    under = jnp.maximum(row_dev - length, 0)
    over_at = jnp.cumsum(over) - over
    under_at = jnp.cumsum(under) - under

    normed = normalize(hidden, norm_gain)
    lane = jnp.arange(TAIL, dtype=jnp.int32)[None, :]
    ids = token_ids[:, None]
    digits = jnp.where(
        lane == 0, ids // 4096, jnp.where(lane == 1, ids // 64 % 64, jnp.where(lane == 2, ids % 64, 0))
    )
    sent = jnp.concatenate([normed, digits.astype(jnp.bfloat16)], axis=1)

    share = row_dev // 2
    slot = t * share + jnp.arange(share, dtype=jnp.int32)
    place = slot % row_dev
    zs = jnp.full((share,), z, jnp.int32)
    own_len = pick(length, zs)
    extra = pick(under_at, zs) + place - own_len
    giver = last_at_or_below(over_at, extra)
    from_back = extra - pick(over_at, giver)
    filled = (place >= own_len)[None, :] & (giver[None, :] == jnp.arange(n_z, dtype=jnp.int32)[:, None])
    row_iota = jnp.arange(row_dev, dtype=jnp.int32)
    select = filled[:, :, None] & (from_back[:, None] == row_iota[None, :])[None]
    select = select.astype(jnp.bfloat16)
    keep = jnp.broadcast_to((place < own_len)[:, None], (share, 128)).astype(jnp.float32)
    full = head_stats(n_dp, n_z, sent, select, keep, head_weight)
    full = full[:, :4].transpose(1, 0, 2).reshape(4, -1)

    row = jnp.arange(row_dev, dtype=jnp.int32)
    zr = jnp.full((row_dev,), z, jnp.int32)
    extra = pick(over_at, zr) + row
    taker = last_at_or_below(under_at, extra)
    back = taker * row_dev + pick(length, taker) + extra - pick(under_at, taker)
    where = jnp.where(core == 0, z * row_dev + row, back)
    scored = core * row_dev + row < pick(length, zr)
    hit = where[:, None] == jnp.arange(n_tensor * share, dtype=jnp.int32)[None, :]
    own = [jnp.sum(jnp.where(hit, full[i][None, :], 0.0), axis=1) for i in range(4)]
    return finish(scored, *own)


def solution(mesh):
    n_dp, n_tensor = mesh.shape["dp"], mesh.shape["tensor"]

    def per_device(hidden, norm_gain, head_weight, token_ids, lengths):
        fits = (
            n_tensor == 2 * SEQ_DP
            and 2 * hidden.shape[0] == SLOT
            and head_weight.shape[1] % (128 * n_dp) == 0
        )
        if not fits:
            return plain_device(hidden, norm_gain, head_weight, token_ids, lengths)
        return kernel_device(n_dp, n_tensor, hidden, norm_gain, head_weight, token_ids, lengths)

    return jax.shard_map(
        per_device,
        mesh=mesh,
        in_specs=(
            P(("dp", "tensor"), None),
            P(),
            P("dp", "tensor"),
            P(("dp", "tensor")),
            P("dp", None),
        ),
        out_specs=(P(("dp", "tensor")), P(("dp", "tensor"))),
        check_vma=False,
    )
```

time: 384 us -> 357 us (0.930)
  Pallas kernels: 244 us -> 346 us
  waiting for transfers between devices: 93.1 us -> 0 us
  blocking collectives: 14 us -> 0 us
  between operations: 14.2 us -> 0.73 us
  matrix products: 5.84 us -> 0 us
    pallas_call x1, Pallas kernels: 244 us -> 346 us  [head_stats(): pl.pallas_call(functools.partial(head_kernel, n_dp, n_z, groups), out_sha...]
    all_gather x1 -> x0, waiting for transfers between devices: 88.3 us -> none  [kernel_device(): everyone = lax.all_gather(sent, 'tensor', axis=0, tiled=True)]
    all_gather x1 -> x0, blocking collectives: 14 us -> none  [kernel_device(): full = merge(lax.all_gather(part, 'tensor', axis=0))]
    dot_general x1 -> x0, matrix products: 5.84 us -> none  [kernel_device(): jnp.dot(chooser.astype(jnp.bfloat16), everyone, preferred_element_type=jn...]
    all_to_all x1 -> x0, waiting for transfers between devices: 4.85 us -> none  [kernel_device(): part = merge(lax.all_to_all(stats, 'dp', 0, 0))]
  transfers between devices with their start and end apart: 2 -> 0, of which waited for: 2 -> 0; matrix products, arithmetic and copies ran while one was open for 0% -> 0% of each run, Pallas kernels for 0% -> 0%
where the time goes in v2:
time: 357 us
  Pallas kernels  346 us (97%)
  other arithmetic  8.2 us (2%)
    pallas_call x1, Pallas kernels, head_stats(): pl.pallas_call(functools.partial(head_kernel, n_dp, n_z, groups), out_sha...  346 us

profile of v2, /device:TPU:0, one launch (start us, length us, event | category | flops | bytes accessed | tf_op | source)
XLA Modules:
  0.0 356.8 jit_solution(13800070298177971718)
XLA Ops:
  0.6 0.7 and_select_fusion.4
  1.3 0.2 select_convert_fusion
  1.5 1.5 fusion
  3.0 0.0 copy-start
  3.1 1.5 fusion.2
  4.6 1.1 pad_maximum_fusion.x_ref
  5.7 0.0 copy-done
  5.7 0.2 reduce-window_clone.1
  5.9 0.2 reduce-window_1_clone.1
  6.1 0.1 select_reduce_fusion.9
  6.2 0.1 convert_reduce_fusion.1
  6.3 0.1 select_reduce_fusion.8
  6.4 0.1 iota_compare_fusion.1
  6.5 0.8 and_convert_fusion.sel_ref
  7.3 0.7 broadcast_in_dim.196.keep_ref
  8.0 346.4 %shard_map.68 = f32[8,8,128]{2,1,0:T(8,128)} custom-call(bf16[256,2176]{1,0:T(8,128)(2,1)} %pad_maximum_fusion.x_ref, bf16[4,128,256]{2,1,0:T(8,128)(2,1)} %and_convert_fusion.sel_ref, f32[128,128]{1,0:T(8,128)} %broadcast_in_dim.196.keep_ref, bf16[512,12800]{1,0:T(8,128)(2,1)} %w_ref.1), custom_call_target="tpu_custom_call" | custom-call | flops 53687091200 | bytes 13107200 | tf_op jit(solution)/shard_map/pallas_call | solution.py:437
  354.5 0.8 slice_bitcast_fusion
  355.3 0.1 select_reduce_fusion.7
  355.4 0.1 convert_reduce_fusion
  355.4 0.1 select_reduce_fusion.5
  355.6 0.7 select_reduce_fusion
  356.3 0.6 subtract_select_fusion
  (15 shorter events, 0.1 us)
Async XLA Ops:
  3.0 2.6 copy-start

commit v3 on v2

--- a/solution.py
+++ b/solution.py
@@ -130,9 +130,8 @@
             w_send.at[g, k - 1], w_recv.at[g, k - 1], (peer, t),
         )
 
-    for g in range(2):
-        for k in range(1, n_dp):
-            weight_copy(g, k, dp).start()
+    for k in range(1, n_dp):
+        weight_copy(0, k, dp).start()
     own_weight = pltpu.make_async_copy(
         w_ref.at[:, pl.ds(pl.multiple_of(dp * vocab, 128), vocab)],
         weight.at[pl.ds(pl.multiple_of(dp * depth, depth), depth)],
@@ -195,53 +194,64 @@
 
     for k in range(1, n_dp):
         plane_copy(k, dp).start()
-
-    def up_copy(d):
-        ref = rows.at[z - d, core]
-        return remote(ref, ref, up_send.at[d], up_recv.at[d], above)
-
-    def down_copy(d):
-        ref = rows.at[z + d, core]
-        return remote(ref, ref, down_send.at[d], down_recv.at[d], below)
+    for g in range(1, len(groups)):
+        for k in range(1, n_dp):
+            weight_copy(g, k, dp).start()
+
+    def share_of(plane, k):
+        at = pl.multiple_of((dp - k + n_dp) % n_dp * share, share)
+        return rows.at[plane, core, pl.ds(at, share)]
+
+    def up_copy(d, k, plane):
+        ref = share_of(plane, k)
+        return remote(ref, ref, up_send.at[d, k], up_recv.at[d, k], above)
+
+    def down_copy(d, k, plane):
+        ref = share_of(plane, k)
+        return remote(ref, ref, down_send.at[d, k], down_recv.at[d, k], below)
 
     def sib_copy(plane, half):
         ref = rows.at[plane, half]
         return remote(ref, ref, sib_send.at[plane], sib_recv.at[plane], sibling)
 
-    for k in range(1, n_dp):
-        plane_copy(k, (dp - k + n_dp) % n_dp).wait_recv()
-
-    @pl.when(z < n_z - 1)
-    def _():
-        up_copy(0).start()
-
-    @pl.when(z > 0)
-    def _():
-        down_copy(0).start()
+    for k in range(n_dp):
+        if k:
+            plane_copy(k, (dp - k + n_dp) % n_dp).wait_recv()
+
+        @pl.when(z < n_z - 1)
+        def _():
+            up_copy(0, k, z).start()
+
+        @pl.when(z > 0)
+        def _():
+            down_copy(0, k, z).start()
 
     sib_copy(z, core).start()
 
     def stage(d):
+        for k in range(n_dp):
+            @pl.when(z >= d)
+            def _():
+                up_copy(d - 1, k, z - d).wait_recv()
+
+                @pl.when(z < n_z - 1)
+                def _():
+                    up_copy(d, k, z - d).start()
+
+            @pl.when(z + d < n_z)
+            def _():
+                down_copy(d - 1, k, z + d).wait_recv()
+
+                @pl.when(z > 0)
+                def _():
+                    down_copy(d, k, z + d).start()
+
         @pl.when(z >= d)
         def _():
-            ref = rows.at[z - d, core]
-            remote(ref, ref, up_send.at[d - 1], up_recv.at[d - 1], above).wait_recv()
-
-            @pl.when(z < n_z - 1)
-            def _():
-                up_copy(d).start()
-
             sib_copy(z - d, core).start()
 
         @pl.when(z + d < n_z)
         def _():
-            ref = rows.at[z + d, core]
-            remote(ref, ref, down_send.at[d - 1], down_recv.at[d - 1], below).wait_recv()
-
-            @pl.when(z > 0)
-            def _():
-                down_copy(d).start()
-
             sib_copy(z + d, core).start()
 
     def wait_weights(g):
@@ -294,13 +304,15 @@
             at += size
 
     near = n_z - 1
-
-    @pl.loop(0, 4 * n_z)
+    last = len(groups) - 1
+
+    @pl.loop(0, 2 * len(groups) * n_z)
     def _(it):
         unit, turn = it // 2, it % 2
         half = (core + turn) % 2
-        second = ((unit >= near) & (unit < 2 * near)) | (unit == 2 * n_z - 1)
-        order = jnp.where(unit < near, unit, jnp.where(unit < 2 * near, unit - near, near))
+        far = unit >= near * len(groups)
+        group = jnp.where(far, unit - near * len(groups), unit // near)
+        order = jnp.where(far, near, unit % near)
         plane = jnp.where(z < n_z // 2, order, n_z - 1 - order)
         entry = plane * 2 + half
 
@@ -308,15 +320,16 @@
         def _():
             stage(2)
 
-        @pl.when(it == 2 * near)
-        def _():
-            wait_weights(1)
-
-        @pl.when(it == 4 * near)
+        for g in range(1, len(groups)):
+            @pl.when(it == 2 * near * g)
+            def _():
+                wait_weights(g)
+
+        @pl.when(it == 2 * near * len(groups))
         def _():
             stage(3)
 
-        @pl.when(jnp.logical_not(second))
+        @pl.when(group == 0)
         def _():
             @pl.when(turn == 1)
             def _():
@@ -325,11 +338,14 @@
             acc[entry, 0] = jnp.full((block, 128), -3e38, jnp.float32)
             for i in range(1, 4):
                 acc[entry, i] = jnp.zeros((block, 128), jnp.float32)
-            multiply(plane, half, 0)
-
-        @pl.when(second)
-        def _():
-            multiply(plane, half, 1)
+
+        for g in range(len(groups)):
+            @pl.when(group == g)
+            def _():
+                multiply(plane, half, g)
+
+        @pl.when(group == last)
+        def _():
             lanes = acc[entry, 0]
             top = jnp.max(lanes, axis=1, keepdims=True)
             scale = jnp.exp(lanes - top)
@@ -388,7 +404,7 @@
     for k in range(1, n_dp):
         plane_copy(k, dp).wait_send()
         stats_dp(k, dp).wait_send()
-        for g in range(2):
+        for g in range(len(groups)):
             weight_copy(g, k, dp).wait_send()
     for k in range(1, n_tensor):
         stats_t(k, t).wait_send()
@@ -407,7 +423,8 @@
     for d in range(n_z - 1):
         @pl.when((z >= d) & (z < n_z - 1))
         def _():
-            up_copy(d).wait_send()
+            for k in range(n_dp):
+                up_copy(d, k, z - d).wait_send()
 
             @pl.when(core == 1)
             def _():
@@ -415,11 +432,18 @@
 
         @pl.when((z + d < n_z) & (z > 0))
         def _():
-            down_copy(d).wait_send()
+            for k in range(n_dp):
+                down_copy(d, k, z + d).wait_send()
 
             @pl.when(core == 1)
             def _():
                 back_down(d).wait_send()
+
+
+def split_columns(vocab):
+    first = vocab * 6 // 25 // 128 * 128
+    second = vocab * 12 // 25 // 128 * 128
+    return [first, second, vocab - first - second]
 
 
 def head_stats(n_dp, n_z, sent, select, keep, head_weight):
@@ -427,9 +451,11 @@
     share = sent.shape[0] // 2
     depth, vocab_dev = head_weight.shape
     width, vocab, block = n_dp * depth, vocab_dev // n_dp, n_dp * share
-    sizes = [512] * (vocab // 512) + ([vocab % 512] if vocab % 512 else [])
-    cut = len(sizes) // 2
-    groups = [(0, sizes[:cut]), (sum(sizes[:cut]), sizes[cut:])]
+    groups, at = [], 0
+    for part in split_columns(vocab):
+        sizes = [min(512, part - done) for done in range(0, part, 512)]
+        groups.append((at, sizes))
+        at += part
     dma = pltpu.SemaphoreType.DMA
     n_tensor = 2 * n_z
     f32, bf16 = jnp.float32, jnp.bfloat16
@@ -452,9 +478,9 @@
             pltpu.VMEM((n_tensor, 8, share), f32),
             pltpu.VMEM((n_tensor, n_tensor, 8, share), f32),
             dma((n_dp - 1,)), dma((n_dp - 1,)),
-            dma((n_z,)), dma((n_z,)), dma((n_z,)), dma((n_z,)),
+            dma((n_z, n_dp)), dma((n_z, n_dp)), dma((n_z, n_dp)), dma((n_z, n_dp)),
             dma((n_z,)), dma((n_z,)),
-            dma((2, n_dp - 1)), dma((2, n_dp - 1)),
+            dma((len(groups), n_dp - 1)), dma((len(groups), n_dp - 1)),
             dma((3,)),
             dma((n_z,)), dma((n_z,)), dma((n_z,)), dma((n_z,)),
             dma((n_z,)), dma((n_z,)),

time: 357 us -> 245 us (0.69)
  Pallas kernels: 346 us -> 235 us
    pallas_call x1, Pallas kernels: 346 us -> 235 us  [head_stats(): pl.pallas_call(functools.partial(head_kernel, n_dp, n_z, groups), out_sha...]
where the time goes in v3:
time: 245 us
  Pallas kernels  235 us (96%)
  other arithmetic  8.2 us (3%)
    pallas_call x1, Pallas kernels, head_stats(): pl.pallas_call(functools.partial(head_kernel, n_dp, n_z, groups), out_sha...  235 us

profile of v3, /device:TPU:0, one launch (start us, length us, event | category | flops | bytes accessed | tf_op | source)
XLA Modules:
  0.0 245.2 jit_solution(11174658595415632464)
XLA Ops:
  0.6 0.7 and_select_fusion.4
  1.3 0.2 select_convert_fusion
  1.5 1.5 fusion
  3.0 0.0 copy-start
  3.1 1.5 fusion.2
  4.6 1.1 pad_maximum_fusion.x_ref
  5.7 0.0 copy-done
  5.7 0.2 reduce-window_clone.1
  5.9 0.2 reduce-window_1_clone.1
  6.1 0.1 select_reduce_fusion.9
  6.2 0.1 convert_reduce_fusion.1
  6.3 0.1 select_reduce_fusion.8
  6.4 0.1 iota_compare_fusion.1
  6.5 0.8 and_convert_fusion.sel_ref
  7.3 0.7 broadcast_in_dim.196.keep_ref
  8.0 234.8 %shard_map.68 = f32[8,8,128]{2,1,0:T(8,128)} custom-call(bf16[256,2176]{1,0:T(8,128)(2,1)} %pad_maximum_fusion.x_ref, bf16[4,128,256]{2,1,0:T(8,128)(2,1)} %and_convert_fusion.sel_ref, f32[128,128]{1,0:T(8,128)} %broadcast_in_dim.196.keep_ref, bf16[512,12800]{1,0:T(8,128)(2,1)} %w_ref.1), custom_call_target="tpu_custom_call" | custom-call | flops 53687091200 | bytes 13107200 | tf_op jit(solution)/shard_map/pallas_call | solution.py:463
  242.8 0.8 slice_bitcast_fusion
  243.6 0.1 select_reduce_fusion.7
  243.7 0.1 convert_reduce_fusion
  243.8 0.1 select_reduce_fusion.5
  243.9 0.7 select_reduce_fusion
  244.6 0.6 subtract_select_fusion
  (15 shorter events, 0.1 us)
Async XLA Ops:
  3.0 2.6 %copy-start = (s32[1,4]{1,0:T(1,128)S(1)}, s32[1,4]{1,0:T(1,128)}, u32[]{:S(2)}) copy-start(s32[1,4]{1,0:T(1,128)} %param.9) | copy-start | bytes 52

commit v4 on v3

--- a/solution.py
+++ b/solution.py
@@ -67,6 +67,7 @@
     sib_send, sib_recv, w_send, w_recv, local_sem,
     bup_send, bup_recv, bdown_send, bdown_recv, bsib_send, bsib_recv,
     front_send, front_recv, sdp_send, sdp_recv, st_send, st_recv,
+    ids_dp, ids_all, idp_send, idp_recv, it_send, it_recv,
 ):
     dp = lax.axis_index("dp")
     t = lax.axis_index("tensor")
@@ -183,7 +184,30 @@
             mine += jnp.dot(
                 sel_ref[plane], back[plane, :, cols], preferred_element_type=jnp.float32
             )
-        rows[z, core, own_at, cols] = mine.astype(jnp.bfloat16)
+        if at < width:
+            rows[z, core, own_at, cols] = mine.astype(jnp.bfloat16)
+            continue
+        lane = lax.broadcasted_iota(jnp.int32, (1, 128), 1)
+        worth = jnp.where(
+            lane == 0, 4096.0, jnp.where(lane == 1, 64.0, jnp.where(lane == 2, 1.0, 0.0))
+        )
+        ids = jnp.sum(mine * worth, axis=1, keepdims=True)
+        ids_dp[dp] = jnp.broadcast_to(ids, (share, 128)).T[:8]
+
+    def ids_dp_copy(k, sender):
+        return remote(
+            ids_dp.at[sender], ids_dp.at[sender],
+            idp_send.at[k - 1], idp_recv.at[k - 1], ((dp + k) % n_dp, t),
+        )
+
+    def ids_t_copy(k, sender):
+        return remote(
+            ids_dp, ids_all.at[sender],
+            it_send.at[k - 1], it_recv.at[k - 1], (dp, (t + k) % n_tensor),
+        )
+
+    for k in range(1, n_dp):
+        ids_dp_copy(k, dp).start()
 
     def plane_copy(k, sender):
         at = pl.ds(pl.multiple_of(sender * share, share), share)
@@ -215,6 +239,12 @@
         return remote(ref, ref, sib_send.at[plane], sib_recv.at[plane], sibling)
 
     for k in range(n_dp):
+        if k == 1:
+            for other in range(1, n_dp):
+                ids_dp_copy(other, (dp - other + n_dp) % n_dp).wait_recv()
+            for other in range(1, n_tensor):
+                ids_t_copy(other, t).start()
+            ids_all[t] = ids_dp[...]
         if k:
             plane_copy(k, (dp - k + n_dp) % n_dp).wait_recv()
 
@@ -261,6 +291,8 @@
     stage(1)
     own_weight.wait()
     wait_weights(0)
+    for k in range(1, n_tensor):
+        ids_t_copy(k, (t - k + n_tensor) % n_tensor).wait_recv()
 
     first = t * (n_dp * vocab) + dp * vocab
     lane = lax.broadcasted_iota(jnp.int32, (1, 128), 1)
@@ -268,13 +300,11 @@
 
     def multiply(plane, half, g):
         entry = plane * 2 + half
-        tail = rows[plane, half, :, width:].astype(jnp.float32)
-        place = jnp.where(
-            lane == 0, 4096.0, jnp.where(lane == 1, 64.0, jnp.where(lane == 2, 1.0, 0.0))
-        )
-        ids = jnp.sum(tail * place, axis=1, keepdims=True).astype(jnp.int32)
-        shifted = ids - first - lane
-        lhs = rows[plane, half, :, :width]
+        shifted = []
+        for i in range(n_dp):
+            ids = jnp.broadcast_to(ids_all[entry, i, 0:1], (128, share)).T
+            shifted.append(ids.astype(jnp.int32) - first - lane)
+        lhs = rows[plane, half]
         at, sizes = groups[g]
         for i, size in enumerate(sizes):
             buf = (buf_a, buf_b)[i % 2]
@@ -283,6 +313,7 @@
             )
             for r in range(0, block, strip):
                 rs = slice(r, r + strip)
+                ids = shifted[r // share][r % share : r % share + strip]
                 tiles = [buf[rs, c : c + 128] for c in range(0, size, 128)]
                 old = acc[entry, 0, rs]
                 top = old
@@ -296,7 +327,7 @@
                     e = jnp.exp(tile - top)
                     total += e
                     moment += e * tile
-                    chosen += jnp.where(shifted[rs] == at + n * 128, tile, 0.0)
+                    chosen += jnp.where(ids == at + n * 128, tile, 0.0)
                 acc[entry, 0, rs] = top
                 acc[entry, 1, rs] = total
                 acc[entry, 2, rs] = moment
@@ -403,11 +434,13 @@
 
     for k in range(1, n_dp):
         plane_copy(k, dp).wait_send()
+        ids_dp_copy(k, dp).wait_send()
         stats_dp(k, dp).wait_send()
         for g in range(len(groups)):
             weight_copy(g, k, dp).wait_send()
     for k in range(1, n_tensor):
         stats_t(k, t).wait_send()
+        ids_t_copy(k, t).wait_send()
     for plane in range(n_z):
         sib_copy(plane, core).wait_send()
 
@@ -441,9 +474,8 @@
 
 
 def split_columns(vocab):
-    first = vocab * 6 // 25 // 128 * 128
-    second = vocab * 12 // 25 // 128 * 128
-    return [first, second, vocab - first - second]
+    parts = [vocab * share // 25 // 128 * 128 for share in (6, 8, 7)]
+    return parts + [vocab - sum(parts)]
 
 
 def head_stats(n_dp, n_z, sent, select, keep, head_weight):
@@ -466,7 +498,7 @@
         in_specs=[vmem, vmem, vmem, pl.BlockSpec(memory_space=pl.ANY)],
         out_specs=vmem,
         scratch_shapes=[
-            pltpu.VMEM((n_z, 2, block, wide), bf16),
+            pltpu.VMEM((n_z, 2, block, width), bf16),
             pltpu.VMEM((width, vocab), bf16),
             pltpu.VMEM((n_z, 2 * share, wide), bf16),
             pltpu.VMEM((share, wide), bf16),
@@ -487,6 +519,10 @@
             dma, dma,
             dma((n_dp - 1,)), dma((n_dp - 1,)),
             dma((n_tensor - 1,)), dma((n_tensor - 1,)),
+            pltpu.VMEM((n_dp, 8, share), f32),
+            pltpu.VMEM((n_tensor, n_dp, 8, share), f32),
+            dma((n_dp - 1,)), dma((n_dp - 1,)),
+            dma((n_tensor - 1,)), dma((n_tensor - 1,)),
         ],
         compiler_params=pltpu.CompilerParams(
             collective_id=0, has_side_effects=True, vmem_limit_bytes=60 * 1024 * 1024

time: 245 us -> 239 us (0.976)
  Pallas kernels: 235 us -> 228 us
    pallas_call x1, Pallas kernels: 235 us -> 228 us  [head_stats(): pl.pallas_call(functools.partial(head_kernel, n_dp, n_z, groups), out_sha...]
where the time goes in v4:
time: 239 us; the launch traced here: 238 us
  Pallas kernels  228 us (95%)
  other arithmetic  8.2 us (3%)
    pallas_call x1, Pallas kernels, head_stats(): pl.pallas_call(functools.partial(head_kernel, n_dp, n_z, groups), out_sha...  228 us

profile of v4, /device:TPU:0, one launch (start us, length us, event | category | flops | bytes accessed | tf_op | source)
XLA Modules:
  0.0 238.4 jit_solution(4317586345245762269)
XLA Ops:
  0.6 0.7 and_select_fusion.4
  1.3 0.2 select_convert_fusion
  1.5 1.5 fusion
  3.0 0.0 copy-start
  3.1 1.5 fusion.2
  4.6 1.1 pad_maximum_fusion.x_ref
  5.7 0.0 copy-done
  5.7 0.2 reduce-window_clone.1
  5.9 0.2 reduce-window_1_clone.1
  6.1 0.1 select_reduce_fusion.9
  6.2 0.1 convert_reduce_fusion.1
  6.3 0.1 select_reduce_fusion.8
  6.4 0.1 iota_compare_fusion.1
  6.5 0.8 and_convert_fusion.sel_ref
  7.3 0.7 broadcast_in_dim.196.keep_ref
  8.0 228.0 %shard_map.68 = f32[8,8,128]{2,1,0:T(8,128)} custom-call(bf16[256,2176]{1,0:T(8,128)(2,1)} %pad_maximum_fusion.x_ref, bf16[4,128,256]{2,1,0:T(8,128)(2,1)} %and_convert_fusion.sel_ref, f32[128,128]{1,0:T(8,128)} %broadcast_in_dim.196.keep_ref, bf16[512,12800]{1,0:T(8,128)(2,1)} %w_ref.1), custom_call_target="tpu_custom_call" | custom-call | flops 53687091200 | bytes 13107200 | tf_op jit(solution)/shard_map/pallas_call | solution.py:495
  236.1 0.8 slice_bitcast_fusion
  236.9 0.1 select_reduce_fusion.7
  237.0 0.1 convert_reduce_fusion
  237.0 0.1 select_reduce_fusion.5
  237.2 0.7 select_reduce_fusion
  237.9 0.6 subtract_select_fusion
  (15 shorter events, 0.1 us)
Async XLA Ops:
  3.0 2.6 %copy-start = (s32[1,4]{1,0:T(1,128)S(1)}, s32[1,4]{1,0:T(1,128)}, u32[]{:S(2)}) copy-start(s32[1,4]{1,0:T(1,128)} %param.9) | copy-start | bytes 52
